TPU v7x, 256 devices: a whole 4x4x8 slice. The times are simulated.
256 devices in a mesh: tx: 16 (over x_lo, y, core), ty: 16 (over x_hi, z).
Axes of the slice: x: 4 (x_hi: 2, x_lo: 2; x = x_hi * 2 + x_lo), y: 4, z: 8, core: 2. Of those that a mesh axis runs over, the one named last changes fastest.
Arguments:
- velocity: float32 [3, 48, 128, 2048], P(None, None, 'tx', 'ty'), may hold values from -6 to 6
- pressure: float32 [48, 128, 2048], P(None, 'tx', 'ty'), may hold values from -6 to 6
- drag_rate: float32 [48, 128, 2048], P(None, 'tx', 'ty'), may hold values from 0.5 to 4
- forcing: float32 [2, 48, 128, 2048], P(None, None, 'tx', 'ty'), may hold values from -6 to 6
- site_velocity: float32 [3, 16, 8, 32768], P(None, None, None, ('tx', 'ty')), may hold values from -6 to 6
- site_pressure: float32 [16, 8, 32768], P(None, None, ('tx', 'ty')), may hold values from -6 to 6
- site_drag: float32 [16, 8, 32768], P(None, None, ('tx', 'ty')), may hold values from 0.5 to 4
- site_forcing: float32 [2, 16, 8, 32768], P(None, None, None, ('tx', 'ty')), may hold values from -6 to 6
- owners: int32 [256], replicated, may hold values from 0 to 9, as said below
- sweep_counts: int32 [10], replicated, may hold values from 3 to 6
- parent_cells: int32 [4096, 1024], P(('tx', 'ty')), may hold values from 0 to 49151
- point_slots: int32 [2, 1114112], P(None, ('tx', 'ty')), may hold values from 0 to 16383
- point_weights: int32 [1114112], P(('tx', 'ty')), may hold values from 0 to 3
Outputs:
- new_velocity: float32 [3, 48, 128, 2048], P(None, None, 'tx', 'ty')
- new_pressure: float32 [48, 128, 2048], P(None, 'tx', 'ty')
- new_site_velocity: float32 [3, 16, 8, 32768], P(None, None, None, ('tx', 'ty'))
- new_site_pressure: float32 [16, 8, 32768], P(None, None, ('tx', 'ty'))
Inputs may be any that keep to these rules, and one draw needn't show every extreme that they name: `owners`: never falls from one device to the next; each of the 10 sites owns one device or more, so its blocks are consecutive. `parent_cells`: row d * 16 + p names a cell of the regional tile at device d's tx index and ty index p, flattened over (height, x, y) within the tile. `point_slots`: the flattened pair p * 1024 + s of the same device's requests. `point_weights`: numerator k of the first parent's weight (2 k + 1) / 8.
All inputs are finite; a program needn't handle non-finite values.
Results may differ from a plain program's by a relative error of at most 0.00002.
Values sent between devices are 32-bit elements; how exact they have to be, the bound alone decides.
A program may use at most 128 MiB of HBM per device.

v0:
```python
import functools

import jax
import jax.numpy as jnp
from jax import lax
from jax.experimental import pallas as pl
from jax.experimental.pallas import tpu as pltpu
from jax.sharding import PartitionSpec as P

F32 = jnp.float32
BF16 = jnp.bfloat16
MESH = pl.DeviceIdType.MESH

NZ = 48
SZ = 16
CAP = 1024
SWEEPS = 8
SSWEEPS = 6
RELAX = 0.3
SIXTH = 1.0 / 6.0
CHUNK = 512
POINTS = 4352
PCHUNK = 256
ZB = 48
FB = 16
EARLY = 4


def one_hot(key, depth):
    n = key.shape[1]
    rows = lax.broadcasted_iota(jnp.int32, (256, n), 0).astype(BF16)
    parts = []
    for b in range(depth // 256):
        low = jnp.where((key >> 8) == b, key & 255, -1) if depth > 256 else key
        low = jnp.broadcast_to(low.astype(F32).astype(BF16), (256, n))
        parts.append(jnp.where(rows == low, jnp.ones((), BF16), jnp.zeros((), BF16)))
    return jnp.concatenate(parts, axis=0) if len(parts) > 1 else parts[0]


def pieces(v):
    hi = v.astype(BF16)
    return hi, (v - hi.astype(F32)).astype(BF16)


def kernel(
    row,
    rows_tx,
    far_vel,
    far_pre,
    far_drag,
    far_forc,
    far_svel,
    far_spre,
    far_sdrag,
    far_sforc,
    owners,
    counts,
    far_cells,
    far_slots,
    far_weights,
    far_out,
    vel,
    pre,
    drag,
    forc,
    svel,
    spre,
    sdrag,
    sforc,
    cells,
    slots,
    weights,
    flat,
    nvel,
    npre,
    nsvel,
    nspre,
    sidx,
    ridx,
    table,
    rep,
    got,
    table2,
    planes,
    xs,
    xr,
    ys,
    yr,
    pred,
    pxs,
    pxr,
    pys,
    pyr,
    src,
    hs,
    hr,
    hm,
    corr,
    step,
    slope,
    sps,
    spr,
    sh,
    wes,
    wer,
    wem,
    load_sem,
    out_sem,
    idx_send,
    idx_recv,
    rep_send,
    rep_recv,
    halo_send,
    halo_recv,
):
    tx = lax.axis_index("tx")
    ty = lax.axis_index("ty")
    me = tx * row + ty
    total = row * rows_tx

    def device(a, b):
        return {"tx": a, "ty": b}

    def place(d):
        return device(d // row, lax.rem(d, row))

    x_before = device(lax.rem(tx + rows_tx - 1, rows_tx), ty)
    x_after = device(lax.rem(tx + 1, rows_tx), ty)
    y_before = device(tx, lax.rem(ty + row - 1, row))
    y_after = device(tx, lax.rem(ty + 1, row))
    d_before = place(lax.rem(me + total - 1, total))
    d_after = place(lax.rem(me + 1, total))

    loads = {}
    for n, (name, far, near) in enumerate(
        (
            ("cells", far_cells, cells),
            ("vel", far_vel, vel),
            ("pre", far_pre, pre),
            ("svel", far_svel, svel),
            ("spre", far_spre, spre),
            ("sdrag", far_sdrag, sdrag),
            ("sforc", far_sforc, sforc),
            ("drag", far_drag, drag),
            ("forc", far_forc, forc),
            ("slots", far_slots, slots),
            ("weights", far_weights, weights),
        )
    ):
        loads[name] = pltpu.make_async_copy(far, near, load_sem.at[n])
        loads[name].start()

    def loaded(*names):
        for name in names:
            loads[name].wait()

    barrier = pltpu.get_barrier_semaphore()
    for t in range(1, row):
        pl.semaphore_signal(
            barrier, inc=1, device_id=device(tx, lax.rem(ty + t, row)), device_id_type=MESH
        )
    for there in (x_before, x_after, d_before, d_after):
        pl.semaphore_signal(barrier, inc=1, device_id=there, device_id_type=MESH)

    lane = lax.broadcasted_iota(jnp.int32, (8, 128), 1)
    sub = lax.broadcasted_iota(jnp.int32, (8, 128), 0)
    zero = jnp.zeros((8, 128), F32)

    def up(v):
        return pltpu.roll(v, 1, v.ndim - 1)

    def down(v):
        return pltpu.roll(v, 127, v.ndim - 1)

    def sub_up(v):
        return pltpu.roll(v, 1, v.ndim - 2)

    def sub_down(v):
        return pltpu.roll(v, 7, v.ndim - 2)

    def copy(src_ref, dst_ref, number, there):
        return pltpu.make_async_remote_copy(
            src_ref=src_ref,
            dst_ref=dst_ref,
            send_sem=halo_send.at[number],
            recv_sem=halo_recv.at[number],
            device_id=there,
            device_id_type=MESH,
        )

    field = [vel.at[0], vel.at[1], vel.at[2], pre]

    loaded("cells")
    for p in range(row):
        sidx[p] = cells[p : p + 1, :]

    loaded("vel", "pre")
    for f in range(4):
        xs[0, f] = field[f][:, 0, :]
        xs[1, f] = field[f][:, 7, :]

    def pack_fields(zz, acc):
        acc = list(acc)
        for f in range(4):
            j = f * 16 + zz
            here = (lane >> 1) == j
            for g in range(3):
                acc[g] = jnp.where(
                    here, pltpu.roll(field[f][g * 16 + zz], 2 * j + 1, 1), acc[g]
                )
        return tuple(acc)

    acc = lax.fori_loop(0, 16, pack_fields, (zero,) * 3)
    for g in range(3):
        ys[g] = acc[g]

    sfield = [svel.at[0], svel.at[1], svel.at[2], spre, sdrag, sforc.at[0], sforc.at[1]]

    loaded("svel", "spre", "sdrag", "sforc")

    def pack_site(j, acc):
        acc = list(acc)
        here = (lane >> 4) == j
        for f in range(7):
            for g in range(2):
                acc[2 * f + g] = jnp.where(
                    here, pltpu.roll(sfield[f][g * 8 + j], 16 * j + 8, 1), acc[2 * f + g]
                )
        return tuple(acc)

    acc = lax.fori_loop(0, 8, pack_site, (zero,) * 14)
    for g in range(14):
        sps[g] = acc[g]

    pl.semaphore_wait(barrier, row - 1 + 4)

    def index_copy(to, slot):
        return pltpu.make_async_remote_copy(
            src_ref=sidx.at[to],
            dst_ref=ridx.at[ty],
            send_sem=idx_send.at[to],
            recv_sem=idx_recv.at[slot],
            device_id=device(tx, to),
            device_id_type=MESH,
        )

    for t in range(1, row):
        index_copy(lax.rem(ty + t, row), ty).start()

    fields_x = [copy(xs.at[0], xr.at[1], 0, x_before), copy(xs.at[1], xr.at[0], 1, x_after)]
    fields_y = [copy(ys, yr.at[1], 2, y_before), copy(ys, yr.at[0], 3, y_after)]
    site_y = [copy(sps, spr.at[1], 4, d_before), copy(sps, spr.at[0], 5, d_after)]
    pred_x = [copy(pxs.at[0], pxr.at[1], 6, x_before), copy(pxs.at[1], pxr.at[0], 7, x_after)]
    pred_y = [copy(pys, pyr.at[1], 8, y_before), copy(pys, pyr.at[0], 9, y_after)]
    src_y = [copy(hs, hr.at[1], 10, y_before), copy(hs, hr.at[0], 11, y_after)]
    src_x = [
        copy(src.at[:, 8:16, 0:128], src.at[:, 16:24, 0:128], 12, x_before),
        copy(src.at[:, 8:16, 0:128], src.at[:, 0:8, 0:128], 13, x_after),
    ]
    corner_x = [copy(hm.at[1], hm.at[2], 14, x_before), copy(hm.at[1], hm.at[0], 15, x_after)]
    plane_y = [copy(wes, wer.at[1], 16, d_before), copy(wes, wer.at[0], 17, d_after)]

    def start(pair):
        for c in pair:
            c.start()

    def arrive(pair):
        for c in pair:
            c.wait_recv()

    start(fields_x)
    start(fields_y)
    start(site_y)

    for f in range(4):
        for x in range(8):
            hi, lo = pieces(field[f][:, x, :])
            table[f * NZ : (f + 1) * NZ, x * 128 : (x + 1) * 128] = hi
            table[(4 + f) * NZ : (5 + f) * NZ, x * 128 : (x + 1) * 128] = lo

    def lookup(q):
        for c in range(CAP // CHUNK):
            v = ridx[q, :, c * CHUNK : (c + 1) * CHUNK]
            found = jnp.dot(table[...], one_hot(v & 1023, 1024), preferred_element_type=F32)
            layer = lax.broadcasted_iota(jnp.int32, (NZ, CHUNK), 0) == (v >> 10)
            for f in range(4):
                s = found[f * NZ : (f + 1) * NZ] + found[(4 + f) * NZ : (5 + f) * NZ]
                s = jnp.sum(jnp.where(layer, s, 0.0), axis=0, keepdims=True)
                for k in range(CHUNK // 128):
                    r = c * (CHUNK // 128) + k
                    rep[q, f, r : r + 1, :] = s[:, k * 128 : (k + 1) * 128]

    def reply_copy(to, slot):
        return pltpu.make_async_remote_copy(
            src_ref=rep.at[to],
            dst_ref=got.at[ty],
            send_sem=rep_send.at[to],
            recv_sem=rep_recv.at[slot],
            device_id=device(tx, to),
            device_id_type=MESH,
        )

    def serve(t, _):
        q = lax.rem(ty + row - t, row)
        index_copy(q, q).wait_recv()
        lookup(q)
        reply_copy(q, ty).start()
        return 0

    ridx[ty] = sidx[ty]
    lookup(ty)
    got[ty] = rep[ty]

    has_x = [jnp.where(tx > 0, 1.0, 0.0), jnp.where(tx < rows_tx - 1, 1.0, 0.0)]
    has_y = [jnp.where(ty > 0, 1.0, 0.0), jnp.where(ty < row - 1, 1.0, 0.0)]
    edge_y = jnp.where(lane < 64, has_y[0], has_y[1])

    lax.fori_loop(1, 4, serve, 0)

    loaded("drag", "forc")
    arrive(fields_x)
    arrive(fields_y)
    for g in range(3):
        first = (lane & 1) == 0
        yr[0, g] = jnp.where(first, down(yr[1, g]), up(yr[0, g]))

    def below(ref, z):
        v = ref[jnp.maximum(z - 1, 0)]
        return v * jnp.where(z > 0, 1.0, 0.0)

    def above(ref, z):
        v = ref[jnp.minimum(z + 1, NZ - 1)]
        return v * jnp.where(z < NZ - 1, 1.0, 0.0)

    def x_sides(v, low, high):
        low = jnp.broadcast_to(low, (8, 128)) * has_x[0]
        high = jnp.broadcast_to(high, (8, 128)) * has_x[1]
        return jnp.where(sub == 0, low, sub_up(v)), jnp.where(sub == 7, high, sub_down(v))

    def y_sides(v, edge):
        edge = edge * edge_y
        return jnp.where(lane == 0, edge, up(v)), jnp.where(lane == 127, edge, down(v))

    def predict(zz, packed):
        for g in range(3):
            z = g * 16 + zz
            inverse = 1.0 / (6.0 + drag[z])
            sides = []
            for f in range(4):
                v = field[f][z]
                xm, xp = x_sides(v, xr[0, f, pl.ds(z, 1), :], xr[1, f, pl.ds(z, 1), :])
                k = 2 * (f * 16 + zz) + 1
                ym, yp = y_sides(v, pltpu.roll(yr[0, g], 128 - k, 1))
                sides.append((xm, xp, ym, yp, below(field[f], z), above(field[f], z)))
            push = sides[3]
            push = [(push[1] - push[0]) * 0.5, (push[3] - push[2]) * 0.5, (push[5] - push[4]) * 0.5]
            out = []
            for i in range(3):
                s = sides[i]
                n = ((s[0] + s[1]) + (s[2] + s[3])) + (s[4] + s[5])
                if i < 2:
                    n = n + forc[i, z]
                out.append((n - push[i]) * inverse)
                pred[i, z] = out[i]
            packed = jnp.where((lane >> 1) == z, pltpu.roll(out[1], 2 * z + 1, 1), packed)
        return packed

    pys[...] = lax.fori_loop(0, 16, predict, zero)
    pxs[0] = pred[0, :, 0, :]
    pxs[1] = pred[0, :, 7, :]
    start(pred_x)
    start(pred_y)

    lax.fori_loop(4, 7, serve, 0)

    arrive(pred_x)
    arrive(pred_y)
    first = (lane & 1) == 0
    edges_v = jnp.where(first, down(pyr[1]), up(pyr[0]))

    def source(j, packed):
        packed = list(packed)
        for g in range(6):
            z = g * 8 + j
            xm, xp = x_sides(pred[0, z], pxr[0, pl.ds(z, 1), :], pxr[1, pl.ds(z, 1), :])
            ym, yp = y_sides(pred[1, z], pltpu.roll(edges_v, 127 - 2 * z, 1))
            div = (xp - xm) + (yp - ym) + (above(pred.at[2], z) - below(pred.at[2], z))
            s = div * 0.5 * (6.0 + drag[z])
            src[z, 8:16, 0:128] = s
            packed[g] = jnp.where((lane >> 4) == j, pltpu.roll(s, 16 * j + 8, 1), packed[g])
        return tuple(packed)

    acc = lax.fori_loop(0, 8, source, (zero,) * 6)
    for g in range(6):
        hs[g] = acc[g]
    start(src_y)

    lax.fori_loop(7, 10, serve, 0)

    arrive(src_y)
    left = ((lane >> 3) & 1) == 0
    for g in range(6):
        hm[1, g] = jnp.where(left, hr[0, g], hr[1, g])
    start(src_x)
    start(corner_x)

    lax.fori_loop(10, row, serve, 0)

    arrive(src_x)
    arrive(corner_x)
    inside = []
    for b in range(3):
        m = (has_x[0], 1.0, has_x[1])[b] * SIXTH
        inside.append(
            jnp.concatenate([jnp.full((8, 128), m, F32), edge_flip(lane, has_y) * m], axis=1)
        )
    inside = jnp.concatenate(inside, axis=0)[None]

    for n in range(2):
        corr[n, 0] = jnp.zeros((40, 256), F32)
        corr[n, NZ + 1] = jnp.zeros((40, 256), F32)
        corr[n, 1 : NZ + 1, 0:8, :] = jnp.zeros((NZ, 8, 256), F32)
        corr[n, 1 : NZ + 1, 32:40, :] = jnp.zeros((NZ, 8, 256), F32)

    def widen(j, _):
        for b in range(3):
            for g in range(6):
                z = g * 8 + j
                s = pltpu.roll(hm[b, g], 120 - 16 * j, 1)
                m = inside[0, 8 * b : 8 * b + 8]
                src[z, 8 * b : 8 * b + 8, 128:256] = s
                corr[1, z + 1, 8 * b + 8 : 8 * b + 16, 0:128] = (
                    -src[z, 8 * b : 8 * b + 8, 0:128] * m[:, :128]
                )
                corr[1, z + 1, 8 * b + 8 : 8 * b + 16, 128:256] = -s * m[:, 128:]
        return 0

    lax.fori_loop(0, 8, widen, 0)

    at = lax.broadcasted_iota(jnp.int32, (256, 256), 0)
    to = lax.broadcasted_iota(jnp.int32, (256, 256), 1)
    after = jnp.where(((at - to) & 255) == 1, 1.0, 0.0)
    before = jnp.where(((to - at) & 255) == 1, 1.0, 0.0)
    both = (after + before).astype(BF16)
    step[0:256, :] = both
    step[256:512, :] = both
    slope[0:256, :] = (after - before)[:, :128].astype(BF16)
    slope[256:512, :] = (after - before)[:, :128].astype(BF16)

    def apply(v, matrix):
        layers, rows, lanes = v.shape
        hi, lo = pieces(v.reshape(layers * rows, lanes))
        out = jnp.dot(
            jnp.concatenate([hi, lo], axis=1), matrix[...], preferred_element_type=F32
        )
        return out.reshape(layers, rows, out.shape[1])

    def sweep(k):
        now, later = k % 2, (k + 1) % 2
        first, rows = (0, 24) if SWEEPS - k > 4 else (4, 16)
        lo, hi = first + 8, first + 8 + rows
        for i in range(NZ // ZB):
            z = i * ZB
            n = apply(corr[now, z + 1 : z + 1 + ZB, lo:hi, :], step)
            n = n + (
                corr[now, z + 1 : z + 1 + ZB, lo - 1 : hi - 1, :]
                + corr[now, z + 1 : z + 1 + ZB, lo + 1 : hi + 1, :]
            )
            n = n + (corr[now, z : z + ZB, lo:hi, :] + corr[now, z + 2 : z + 2 + ZB, lo:hi, :])
            n = n - src[z : z + ZB, first : first + rows, :]
            corr[later, z + 1 : z + 1 + ZB, lo:hi, :] = n * inside[:, first : first + rows]

    for k in range(1, EARLY):
        sweep(k)

    loaded("slots", "weights")
    flat[...] = weights[...].reshape(1, POINTS)
    for t in range(1, row):
        q = lax.rem(ty + row - t, row)
        reply_copy(q, q).wait_recv()
    for f in range(4):
        for b in range(2):
            for u in range(row // 4):
                v = jnp.concatenate([got[4 * u + b, f], got[4 * u + 2 + b, f]], axis=0)
                hi, lo = pieces(v)
                r = f * 4 * row + u * 16
                table2[r : r + 16, b * 128 : (b + 1) * 128] = hi
                table2[16 * row + r : 16 * row + r + 16, b * 128 : (b + 1) * 128] = lo

    def point(c, _):
        at = pl.ds(pl.multiple_of(c * PCHUNK, PCHUNK), PCHUNK)
        j = jnp.concatenate([slots[0:1, at], slots[1:2, at]], axis=1)
        key = (j & 127) | (((j >> 10) & 1) << 7)
        m = ((j >> 11) << 3) | ((j >> 7) & 7)
        found = jnp.dot(table2[...], one_hot(key, 256), preferred_element_type=F32)
        here = lax.broadcasted_iota(jnp.int32, (4 * row, 2 * PCHUNK), 0) == m
        w = (2.0 * flat[:, at].astype(F32) + 1.0) * 0.125
        for f in range(4):
            r = f * 4 * row
            s = found[r : r + 4 * row] + found[16 * row + r : 16 * row + r + 4 * row]
            s = jnp.sum(jnp.where(here, s, 0.0), axis=0, keepdims=True)
            v = w * s[:, :PCHUNK] + (1.0 - w) * s[:, PCHUNK:]
            planes[f, pl.ds(2 * c, 1), :] = v[:, :128]
            planes[f, pl.ds(2 * c + 1, 1), :] = v[:, 128:]
        return 0

    lax.fori_loop(0, POINTS // PCHUNK, point, 0)

    acc = [zero, zero]
    for n in range(16):
        v = planes[n // 4, (n % 4) * 8 : (n % 4) * 8 + 8, :]
        j = n % 8
        acc[n // 8] = jnp.where((lane >> 4) == j, pltpu.roll(v, 16 * j + 8, 1), acc[n // 8])
    wes[0] = acc[0]
    wes[1] = acc[1]
    start(plane_y)

    for k in range(EARLY, SWEEPS):
        sweep(k)
    last = SWEEPS % 2

    def finish(i, _):
        z = i * FB
        c = corr[last, pl.ds(z + 1, FB), 16:24, :]
        gy = apply(c, slope)
        gx = corr[last, pl.ds(z + 1, FB), 17:25, :128] - corr[last, pl.ds(z + 1, FB), 15:23, :128]
        gz = corr[last, pl.ds(z + 2, FB), 16:24, :128] - corr[last, pl.ds(z, FB), 16:24, :128]
        half = 0.5 / (6.0 + drag[pl.ds(z, FB)])
        nvel[0, pl.ds(z, FB)] = pred[0, pl.ds(z, FB)] - gx * half
        nvel[1, pl.ds(z, FB)] = pred[1, pl.ds(z, FB)] - gy * half
        nvel[2, pl.ds(z, FB)] = pred[2, pl.ds(z, FB)] - gz * half
        npre[pl.ds(z, FB)] = pre[pl.ds(z, FB)] + RELAX * c[:, :, :128]
        return 0

    lax.fori_loop(0, NZ // FB, finish, 0)

    stores = []
    for n in range(8):
        near = (nvel.at[0], nvel.at[1], nvel.at[2], npre, nsvel.at[0], nsvel.at[1], nsvel.at[2], nspre)[n]
        first = n * NZ if n < 4 else 4 * NZ + (n - 4) * SZ
        size = NZ if n < 4 else SZ
        stores.append(pltpu.make_async_copy(near, far_out.at[first : first + size], out_sem.at[n]))
    for n in range(4):
        stores[n].start()

    own = owners[me]
    begins = (me == 0) | (owners[jnp.maximum(me - 1, 0)] != own)
    ends = (me == total - 1) | (owners[jnp.minimum(me + 1, total - 1)] != own)
    begins = jnp.full((8, 128), begins.astype(F32), F32)
    ends = jnp.full((8, 128), ends.astype(F32), F32)
    allowed = jnp.full((8, 128), counts[own], jnp.int32)
    other = jnp.where(lane < 64, ends, begins) > 0.5

    def ends_of(f):
        s = jnp.where((lane & 7) == sub, jnp.broadcast_to(planes[f, 32:33, :], (8, 128)), 0.0)
        n = jnp.where((lane & 7) == sub, jnp.broadcast_to(planes[f, 33:34, :], (8, 128)), 0.0)
        for k in (1, 2, 4):
            s = s + pltpu.roll(s, k, 1)
            n = n + pltpu.roll(n, 128 - k, 1)
        both = jnp.where((lane & 7) == 7, s, pltpu.roll(n, 8, 1))
        return [pltpu.roll(both, (120 - 8 * z) % 128, 1) for z in range(SZ)]

    outer = [jnp.stack(ends_of(f)) for f in range(4)]
    edge_lane = (lane == 0) | (lane == 127)

    def with_ends(v, f):
        return jnp.where((edge_lane & other)[None], outer[f], v)

    arrive(site_y)
    arrive(plane_y)
    left = ((lane >> 3) & 1) == 0
    for g in range(14):
        spr[0, g] = jnp.where(left, spr[0, g], spr[1, g])
    for n in range(7 * SZ):
        sh[n // SZ, n % SZ] = pltpu.roll(spr[0, n // 8], (120 - 16 * (n % 8)) % 128, 1)
    for g in range(2):
        v = jnp.where(left, wer[0, g], wer[1, g])
        for j in range(8):
            n = g * 8 + j
            wem[n // 4, (n % 4) * 8 : (n % 4) * 8 + 8, :] = pltpu.roll(v, (120 - 16 * j) % 128, 1)

    west = [[planes[f, 0:SZ, :], wem[f, 0:SZ, :]] for f in range(4)]
    east = [[planes[f, SZ : 2 * SZ, :], wem[f, SZ : 2 * SZ, :]] for f in range(4)]

    def layer_sides(v):
        blank = jnp.zeros((1, 8, 128), F32)
        return jnp.concatenate([blank, v[:-1]], axis=0), jnp.concatenate([v[1:], blank], axis=0)

    def site_x(v, h, f):
        shape = (SZ, 8, 128)
        if f is None:
            low = high = jnp.zeros(shape, F32)
        else:
            low = jnp.broadcast_to(west[f][h][:, None, :], shape)
            high = jnp.broadcast_to(east[f][h][:, None, :], shape)
        return jnp.where(sub[None] == 0, low, sub_up(v)), jnp.where(sub[None] == 7, high, sub_down(v))

    def site_y_sides(pair):
        u = [up(v) for v in pair]
        d = [down(v) for v in pair]
        return [
            (
                jnp.where(lane[None] == 0, u[1 - h], u[h]),
                jnp.where(lane[None] == 127, d[1 - h], d[h]),
            )
            for h in range(2)
        ]

    fields = [[sfield[f][...], with_ends(sh[f], f)] for f in range(4)]
    diag = [6.0 + sdrag[...], 6.0 + sh[4]]
    inverse = [1.0 / v for v in diag]
    force = [[sforc[i], sh[5 + i]] for i in range(2)]
    xside = [[site_x(fields[f][h], h, f) for h in range(2)] for f in range(4)]
    yside = [site_y_sides(fields[f]) for f in range(4)]
    moved = [[None, None] for _ in range(3)]
    for h in range(2):
        below_p, above_p = layer_sides(fields[3][h])
        push = [
            (xside[3][h][1] - xside[3][h][0]) * 0.5,
            (yside[3][h][1] - yside[3][h][0]) * 0.5,
            (above_p - below_p) * 0.5,
        ]
        for i in range(3):
            lo, hi = layer_sides(fields[i][h])
            n = (xside[i][h][0] + xside[i][h][1]) + (yside[i][h][0] + yside[i][h][1]) + (lo + hi)
            if i < 2:
                n = n + force[i][h]
            v = (n - push[i]) * inverse[h]
            moved[i][h] = with_ends(v, i) if h == 1 else v

    ys_v = site_y_sides(moved[1])
    term = []
    for h in range(2):
        xm, xp = site_x(moved[0][h], h, 0)
        lo, hi = layer_sides(moved[2][h])
        term.append(((xp - xm) + (ys_v[h][1] - ys_v[h][0]) + (hi - lo)) * 0.5 * diag[h])

    keep = [
        jnp.full((1, 8, 128), SIXTH, F32),
        jnp.where(other, 0.0, SIXTH)[None],
    ]
    e = [-term[h] * keep[h] for h in range(2)]
    for k in range(1, SSWEEPS):
        sides = site_y_sides(e)
        fresh = []
        for h in range(2):
            xm, xp = site_x(e[h], h, None)
            lo, hi = layer_sides(e[h])
            n = (xm + xp) + (sides[h][0] + sides[h][1]) + (lo + hi)
            fresh.append(jnp.where((allowed > k)[None], (n - term[h]) * keep[h], e[h]))
        e = fresh
    xm, xp = site_x(e[0], 0, None)
    ym, yp = site_y_sides(e)[0]
    lo, hi = layer_sides(e[0])
    half = 0.5 * inverse[0]
    nsvel[0] = moved[0][0] - (xp - xm) * half
    nsvel[1] = moved[1][0] - (yp - ym) * half
    nsvel[2] = moved[2][0] - (hi - lo) * half
    nspre[...] = spre[...] + RELAX * e[0]

    for n in range(4, 8):
        stores[n].start()

    for pair in (fields_x, fields_y, site_y, pred_x, pred_y, src_y, src_x, corner_x, plane_y):
        for c in pair:
            c.wait_send()
    for t in range(1, row):
        q = lax.rem(ty + t, row)
        index_copy(q, q).wait_send()
        reply_copy(q, q).wait_send()
    for c in stores:
        c.wait()


def spread(far, nvel, npre, nsvel, nspre, held, sem):
    places = (nvel.at[0], nvel.at[1], nvel.at[2], npre)
    places += (nsvel.at[0], nsvel.at[1], nsvel.at[2], nspre)
    first, moves = 0, []
    for n, place in enumerate(places):
        part = pl.ds(first, place.shape[0])
        moves.append(
            (
                pltpu.make_async_copy(far.at[part], held.at[part], sem.at[0, n]),
                pltpu.make_async_copy(held.at[part], place, sem.at[1, n]),
            )
        )
        first += place.shape[0]
    for come, _ in moves:
        come.start()
    for come, go in moves:
        come.wait()
        go.start()
    for _, go in moves:
        go.wait()


def edge_flip(lane, has_y):
    return jnp.where(lane < 64, has_y[1], has_y[0])


def shards(
    velocity,
    pressure,
    drag_rate,
    forcing,
    site_velocity,
    site_pressure,
    site_drag,
    site_forcing,
    owners,
    sweep_counts,
    parent_cells,
    point_slots,
    point_weights,
):
    row = lax.axis_size("ty")
    rows_tx = lax.axis_size("tx")
    sm = pl.BlockSpec(memory_space=pltpu.SMEM)
    hbm = pl.BlockSpec(memory_space=pl.ANY)

    def v(*shape):
        return pltpu.VMEM(shape, F32)

    both = pl.pallas_call(
        functools.partial(kernel, row, rows_tx),
        out_shape=jax.ShapeDtypeStruct((4 * (NZ + SZ), 8, 128), F32),
        in_specs=[hbm] * 8 + [sm] * 2 + [hbm] * 3,
        out_specs=hbm,
        scratch_shapes=[
            v(3, NZ, 8, 128),
            v(NZ, 8, 128),
            v(NZ, 8, 128),
            v(2, NZ, 8, 128),
            v(3, SZ, 8, 128),
            v(SZ, 8, 128),
            v(SZ, 8, 128),
            v(2, SZ, 8, 128),
            pltpu.VMEM((row, CAP), jnp.int32),
            pltpu.VMEM((2, POINTS), jnp.int32),
            pltpu.VMEM((POINTS,), jnp.int32),
            pltpu.VMEM((1, POINTS), jnp.int32),
            v(3, NZ, 8, 128),
            v(NZ, 8, 128),
            v(3, SZ, 8, 128),
            v(SZ, 8, 128),
            pltpu.VMEM((row, 1, CAP), jnp.int32),
            pltpu.VMEM((row, 1, CAP), jnp.int32),
            pltpu.VMEM((8 * NZ, 1024), BF16),
            v(row, 4, 8, 128),
            v(row, 4, 8, 128),
            pltpu.VMEM((32 * row, 256), BF16),
            v(4, 40, 128),
            v(2, 4, NZ, 128),
            v(2, 4, NZ, 128),
            v(3, 8, 128),
            v(2, 3, 8, 128),
            v(3, NZ, 8, 128),
            v(2, NZ, 128),
            v(2, NZ, 128),
            v(8, 128),
            v(2, 8, 128),
            v(NZ, 24, 256),
            v(6, 8, 128),
            v(2, 6, 8, 128),
            v(3, 6, 8, 128),
            v(2, NZ + 2, 40, 256),
            pltpu.VMEM((512, 256), BF16),
            pltpu.VMEM((512, 128), BF16),
            v(14, 8, 128),
            v(2, 14, 8, 128),
            v(7, SZ, 8, 128),
            v(2, 8, 128),
            v(2, 2, 8, 128),
            v(4, 2 * SZ, 128),
            pltpu.SemaphoreType.DMA((11,)),
            pltpu.SemaphoreType.DMA((8,)),
            pltpu.SemaphoreType.DMA((row,)),
            pltpu.SemaphoreType.DMA((row,)),
            pltpu.SemaphoreType.DMA((row,)),
            pltpu.SemaphoreType.DMA((row,)),
            pltpu.SemaphoreType.DMA((18,)),
            pltpu.SemaphoreType.DMA((18,)),
        ],
        compiler_params=pltpu.CompilerParams(
            collective_id=0, has_side_effects=True, vmem_limit_bytes=60 * 2**20
        ),
        name="wind_step",
    )(
        velocity,
        pressure,
        drag_rate,
        forcing,
        site_velocity,
        site_pressure,
        site_drag,
        site_forcing,
        owners,
        sweep_counts,
        parent_cells,
        point_slots,
        point_weights,
    )
    return pl.pallas_call(
        spread,
        out_shape=[
            jax.ShapeDtypeStruct(a.shape, F32)
            for a in (velocity, pressure, site_velocity, site_pressure)
        ],
        in_specs=[hbm],
        out_specs=[hbm] * 4,
        scratch_shapes=[v(4 * (NZ + SZ), 8, 128), pltpu.SemaphoreType.DMA((2, 8))],
        name="spread",
    )(both)


def solution(mesh):
    placed = (
        P(None, None, "tx", "ty"),
        P(None, "tx", "ty"),
        P(None, "tx", "ty"),
        P(None, None, "tx", "ty"),
        P(None, None, None, ("tx", "ty")),
        P(None, None, ("tx", "ty")),
        P(None, None, ("tx", "ty")),
        P(None, None, None, ("tx", "ty")),
        P(),
        P(),
        P(("tx", "ty"), None),
        P(None, ("tx", "ty")),
        P(("tx", "ty")),
    )
    return jax.shard_map(
        shards,
        mesh=mesh,
        in_specs=placed,
        out_specs=(
            P(None, None, "tx", "ty"),
            P(None, "tx", "ty"),
            P(None, None, None, ("tx", "ty")),
            P(None, None, ("tx", "ty")),
        ),
        check_vma=False,
    )
```

profile of v0, /device:TPU:2, one launch (start us, length us, event | category | flops | bytes accessed | tf_op | source)
XLA Modules:
  0.0 54.9 jit_solution(6191401950675475513)
XLA Ops:
  0.6 52.2 %wind_step.1.far = f32[256,8,128]{2,1,0:T(8,128)} custom-call(f32[3,48,8,128]{3,2,1,0:T(8,128)} %far_vel.1, f32[48,8,128]{2,1,0:T(8,128)} %far_pre.1, f32[48,8,128]{2,1,0:T(8,128)} %far_drag.1, f32[2,48,8,128]{3,2,1,0:T(8,128)} %far_forc.1, f32[3,16,8,128]{3,2,1,0:T(8,128)} %far_svel.1, f32[16,8,128]{2,1,0:T(8,128)} %far_spre.1, f32[16,8,128]{2,1,0:T(8,128)} %far_sdrag.1, ...), custom_call_target="tpu_custom_call" | custom-call | tf_op jit(solution)/shard_map/wind_step/pallas_call | solution.py:724
  52.8 2.1 %spread.1 = (f32[3,48,8,128]{3,2,1,0:T(8,128)}, f32[48,8,128]{2,1,0:T(8,128)}, f32[3,16,8,128]{3,2,1,0:T(8,128)}, f32[16,8,128]{2,1,0:T(8,128)}) custom-call(f32[256,8,128]{2,1,0:T(8,128)} %wind_step.1.far), custom_call_target="tpu_custom_call" | custom-call | tf_op jit(solution)/shard_map/spread/pallas_call | solution.py:803
where the time goes:
time: 55.6 us; the launch traced here: 54.9 us
  Pallas kernels  54.3 us (98%)
  between operations  0.64 us (1%)
    pallas_call x1, Pallas kernels, shards(): pl.pallas_call(functools.partial(kernel, row, rows_tx), out_shape=jax.Sha...  52.2 us
    pallas_call x1, Pallas kernels, shards(): pl.pallas_call(spread, out_shape=[jax.ShapeDtypeStruct(a.shape, F32) for...  2.12 us

commit v1 on v0

--- a/solution.py
+++ b/solution.py
@@ -23,7 +23,7 @@
 PCHUNK = 256
 ZB = 48
 FB = 16
-EARLY = 4
+EARLY = 5
 
 
 def one_hot(key, depth):
@@ -94,6 +94,7 @@
     src,
     hs,
     hr,
+    hd,
     hm,
     corr,
     step,
@@ -104,6 +105,8 @@
     wes,
     wer,
     wem,
+    rows,
+    rim,
     load_sem,
     out_sem,
     idx_send,
@@ -154,17 +157,24 @@
         for name in names:
             loads[name].wait()
 
+    diagonal = [
+        device(there["tx"], side["ty"])
+        for there in (x_before, x_after)
+        for side in (y_before, y_after)
+    ]
+
     barrier = pltpu.get_barrier_semaphore()
     for t in range(1, row):
         pl.semaphore_signal(
             barrier, inc=1, device_id=device(tx, lax.rem(ty + t, row)), device_id_type=MESH
         )
-    for there in (x_before, x_after, d_before, d_after):
+    for there in (x_before, x_after, d_before, d_after, *diagonal):
         pl.semaphore_signal(barrier, inc=1, device_id=there, device_id_type=MESH)
 
     lane = lax.broadcasted_iota(jnp.int32, (8, 128), 1)
     sub = lax.broadcasted_iota(jnp.int32, (8, 128), 0)
     zero = jnp.zeros((8, 128), F32)
+    left = ((lane >> 3) & 1) == 0
 
     def up(v):
         return pltpu.roll(v, 1, v.ndim - 1)
@@ -232,7 +242,7 @@
     for g in range(14):
         sps[g] = acc[g]
 
-    pl.semaphore_wait(barrier, row - 1 + 4)
+    pl.semaphore_wait(barrier, row - 1 + 8)
 
     def index_copy(to, slot):
         return pltpu.make_async_remote_copy(
@@ -257,8 +267,10 @@
         copy(src.at[:, 8:16, 0:128], src.at[:, 16:24, 0:128], 12, x_before),
         copy(src.at[:, 8:16, 0:128], src.at[:, 0:8, 0:128], 13, x_after),
     ]
-    corner_x = [copy(hm.at[1], hm.at[2], 14, x_before), copy(hm.at[1], hm.at[0], 15, x_after)]
-    plane_y = [copy(wes, wer.at[1], 16, d_before), copy(wes, wer.at[0], 17, d_after)]
+    corner_x = [
+        copy(hs, hd.at[1 - n // 2, 1 - n % 2], 14 + n, diagonal[n]) for n in range(4)
+    ]
+    plane_y = [copy(wes, wer.at[1], 18, d_before), copy(wes, wer.at[0], 19, d_after)]
 
     def start(pair):
         for c in pair:
@@ -273,16 +285,21 @@
     start(site_y)
 
     for f in range(4):
-        for x in range(8):
-            hi, lo = pieces(field[f][:, x, :])
-            table[f * NZ : (f + 1) * NZ, x * 128 : (x + 1) * 128] = hi
-            table[(4 + f) * NZ : (5 + f) * NZ, x * 128 : (x + 1) * 128] = lo
+        for u in range(NZ // 16):
+            for k in range(8):
+                z = 16 * u + k
+                hi, lo = pieces(jnp.concatenate([field[f][z], field[f][z + 8]], axis=0))
+                r = f * NZ + 16 * u
+                table[r : r + 16, k * 128 : (k + 1) * 128] = hi
+                table[4 * NZ + r : 4 * NZ + r + 16, k * 128 : (k + 1) * 128] = lo
 
     def lookup(q):
         for c in range(CAP // CHUNK):
             v = ridx[q, :, c * CHUNK : (c + 1) * CHUNK]
-            found = jnp.dot(table[...], one_hot(v & 1023, 1024), preferred_element_type=F32)
-            layer = lax.broadcasted_iota(jnp.int32, (NZ, CHUNK), 0) == (v >> 10)
+            key = (v & 127) | (((v >> 10) & 7) << 7)
+            m = ((v >> 13) << 3) | ((v >> 7) & 7)
+            found = jnp.dot(table[...], one_hot(key, 1024), preferred_element_type=F32)
+            layer = lax.broadcasted_iota(jnp.int32, (NZ, CHUNK), 0) == m
             for f in range(4):
                 s = found[f * NZ : (f + 1) * NZ] + found[(4 + f) * NZ : (5 + f) * NZ]
                 s = jnp.sum(jnp.where(layer, s, 0.0), axis=0, keepdims=True)
@@ -311,11 +328,33 @@
     lookup(ty)
     got[ty] = rep[ty]
 
+    def open_site():
+        for g in range(14):
+            spr[0, g] = jnp.where(left, spr[0, g], spr[1, g])
+        for n in range(7 * SZ):
+            sh[n // SZ, n % SZ] = pltpu.roll(spr[0, n // 8], (120 - 16 * (n % 8)) % 128, 1)
+
+    def open_slots():
+        loaded("slots", "weights")
+        flat[...] = weights[...].reshape(1, POINTS)
+        for n in range(2 * SZ):
+            at = pl.ds(n * 128, 128)
+            rows[0, n : n + 1, :] = slots[0:1, at]
+            rows[1, n : n + 1, :] = slots[1:2, at]
+            rows[2, n : n + 1, :] = flat[:, at]
+        for r in range(3):
+            v = jnp.zeros((8, 128), jnp.int32)
+            for g in range(4):
+                v = jnp.where(
+                    (lane >> 4) == g, pltpu.roll(rows[r, 8 * g : 8 * g + 8, :], 16 * g + 8, 1), v
+                )
+            rim[r] = v
+
     has_x = [jnp.where(tx > 0, 1.0, 0.0), jnp.where(tx < rows_tx - 1, 1.0, 0.0)]
     has_y = [jnp.where(ty > 0, 1.0, 0.0), jnp.where(ty < row - 1, 1.0, 0.0)]
     edge_y = jnp.where(lane < 64, has_y[0], has_y[1])
 
-    lax.fori_loop(1, 4, serve, 0)
+    lax.fori_loop(1, 3, serve, 0)
 
     loaded("drag", "forc")
     arrive(fields_x)
@@ -365,13 +404,19 @@
             packed = jnp.where((lane >> 1) == z, pltpu.roll(out[1], 2 * z + 1, 1), packed)
         return packed
 
-    pys[...] = lax.fori_loop(0, 16, predict, zero)
+    def serve_predict(i, packed):
+        serve(3 + i, 0)
+        for zz in range(8):
+            packed = predict(i * 8 + zz, packed)
+        return packed
+
+    pys[...] = lax.fori_loop(0, 2, serve_predict, zero)
     pxs[0] = pred[0, :, 0, :]
     pxs[1] = pred[0, :, 7, :]
     start(pred_x)
     start(pred_y)
 
-    lax.fori_loop(4, 7, serve, 0)
+    lax.fori_loop(5, 8, serve, 0)
 
     arrive(pred_x)
     arrive(pred_y)
@@ -390,24 +435,32 @@
             packed[g] = jnp.where((lane >> 4) == j, pltpu.roll(s, 16 * j + 8, 1), packed[g])
         return tuple(packed)
 
-    acc = lax.fori_loop(0, 8, source, (zero,) * 6)
+    serve(8, 0)
+    acc = (zero,) * 6
+    for j in range(8):
+        acc = source(j, acc)
     for g in range(6):
         hs[g] = acc[g]
     start(src_y)
-
-    lax.fori_loop(7, 10, serve, 0)
+    start(corner_x)
+    start(src_x)
+
+    serve(9, 0)
+    open_slots()
+    serve(10, 0)
+    arrive(site_y)
+    serve(11, 0)
+    open_site()
+    serve(12, 0)
 
     arrive(src_y)
-    left = ((lane >> 3) & 1) == 0
+    arrive(corner_x)
     for g in range(6):
+        hm[0, g] = jnp.where(left, hd[0, 0, g], hd[0, 1, g])
         hm[1, g] = jnp.where(left, hr[0, g], hr[1, g])
-    start(src_x)
-    start(corner_x)
-
-    lax.fori_loop(10, row, serve, 0)
+        hm[2, g] = jnp.where(left, hd[1, 0, g], hd[1, 1, g])
 
     arrive(src_x)
-    arrive(corner_x)
     inside = []
     for b in range(3):
         m = (has_x[0], 1.0, has_x[1])[b] * SIXTH
@@ -435,7 +488,10 @@
                 corr[1, z + 1, 8 * b + 8 : 8 * b + 16, 128:256] = -s * m[:, 128:]
         return 0
 
-    lax.fori_loop(0, 8, widen, 0)
+    serve(13, 0)
+    for j in range(8):
+        widen(j, 0)
+    lax.fori_loop(14, row, serve, 0)
 
     at = lax.broadcasted_iota(jnp.int32, (256, 256), 0)
     to = lax.broadcasted_iota(jnp.int32, (256, 256), 1)
@@ -473,8 +529,6 @@
     for k in range(1, EARLY):
         sweep(k)
 
-    loaded("slots", "weights")
-    flat[...] = weights[...].reshape(1, POINTS)
     for t in range(1, row):
         q = lax.rem(ty + row - t, row)
         reply_copy(q, q).wait_recv()
@@ -487,35 +541,38 @@
                 table2[r : r + 16, b * 128 : (b + 1) * 128] = hi
                 table2[16 * row + r : 16 * row + r + 16, b * 128 : (b + 1) * 128] = lo
 
-    def point(c, _):
-        at = pl.ds(pl.multiple_of(c * PCHUNK, PCHUNK), PCHUNK)
-        j = jnp.concatenate([slots[0:1, at], slots[1:2, at]], axis=1)
+    def point(j, w):
+        n = w.shape[1]
         key = (j & 127) | (((j >> 10) & 1) << 7)
         m = ((j >> 11) << 3) | ((j >> 7) & 7)
         found = jnp.dot(table2[...], one_hot(key, 256), preferred_element_type=F32)
-        here = lax.broadcasted_iota(jnp.int32, (4 * row, 2 * PCHUNK), 0) == m
-        w = (2.0 * flat[:, at].astype(F32) + 1.0) * 0.125
+        here = lax.broadcasted_iota(jnp.int32, (4 * row, 2 * n), 0) == m
+        w = (2.0 * w.astype(F32) + 1.0) * 0.125
+        out = []
         for f in range(4):
             r = f * 4 * row
             s = found[r : r + 4 * row] + found[16 * row + r : 16 * row + r + 4 * row]
             s = jnp.sum(jnp.where(here, s, 0.0), axis=0, keepdims=True)
-            v = w * s[:, :PCHUNK] + (1.0 - w) * s[:, PCHUNK:]
-            planes[f, pl.ds(2 * c, 1), :] = v[:, :128]
-            planes[f, pl.ds(2 * c + 1, 1), :] = v[:, 128:]
-        return 0
-
-    lax.fori_loop(0, POINTS // PCHUNK, point, 0)
-
-    acc = [zero, zero]
-    for n in range(16):
-        v = planes[n // 4, (n % 4) * 8 : (n % 4) * 8 + 8, :]
-        j = n % 8
-        acc[n // 8] = jnp.where((lane >> 4) == j, pltpu.roll(v, 16 * j + 8, 1), acc[n // 8])
-    wes[0] = acc[0]
-    wes[1] = acc[1]
+            out.append(w * s[:, :n] + (1.0 - w) * s[:, n:])
+        return out
+
+    for c in range(4):
+        r = [rim[k, 2 * c + i : 2 * c + i + 1, :] for k in range(3) for i in range(2)]
+        out = point(jnp.concatenate(r[:4], axis=1), jnp.concatenate(r[4:], axis=1))
+        for f in range(4):
+            wes[f, 2 * c : 2 * c + 1, :] = out[f][:, :128]
+            wes[f, 2 * c + 1 : 2 * c + 2, :] = out[f][:, 128:]
     start(plane_y)
 
-    for k in range(EARLY, SWEEPS):
+    for c in range(POINTS // PCHUNK):
+        at = pl.ds(c * PCHUNK, PCHUNK)
+        out = point(jnp.concatenate([slots[0:1, at], slots[1:2, at]], axis=1), flat[:, at])
+        for f in range(4):
+            planes[f, 2 * c : 2 * c + 1, :] = out[f][:, :128]
+            planes[f, 2 * c + 1 : 2 * c + 2, :] = out[f][:, 128:]
+    sweep(EARLY)
+
+    for k in range(EARLY + 1, SWEEPS):
         sweep(k)
     last = SWEEPS % 2
 
@@ -566,18 +623,11 @@
     def with_ends(v, f):
         return jnp.where((edge_lane & other)[None], outer[f], v)
 
-    arrive(site_y)
     arrive(plane_y)
-    left = ((lane >> 3) & 1) == 0
-    for g in range(14):
-        spr[0, g] = jnp.where(left, spr[0, g], spr[1, g])
-    for n in range(7 * SZ):
-        sh[n // SZ, n % SZ] = pltpu.roll(spr[0, n // 8], (120 - 16 * (n % 8)) % 128, 1)
-    for g in range(2):
-        v = jnp.where(left, wer[0, g], wer[1, g])
-        for j in range(8):
-            n = g * 8 + j
-            wem[n // 4, (n % 4) * 8 : (n % 4) * 8 + 8, :] = pltpu.roll(v, (120 - 16 * j) % 128, 1)
+    for f in range(4):
+        v = jnp.where(left, wer[0, f], wer[1, f])
+        for g in range(4):
+            wem[f, 8 * g : 8 * g + 8, :] = pltpu.roll(v, 120 - 16 * g, 1)
 
     west = [[planes[f, 0:SZ, :], wem[f, 0:SZ, :]] for f in range(4)]
     east = [[planes[f, SZ : 2 * SZ, :], wem[f, SZ : 2 * SZ, :]] for f in range(4)]
@@ -762,6 +812,7 @@
             v(NZ, 24, 256),
             v(6, 8, 128),
             v(2, 6, 8, 128),
+            v(2, 2, 6, 8, 128),
             v(3, 6, 8, 128),
             v(2, NZ + 2, 40, 256),
             pltpu.VMEM((512, 256), BF16),
@@ -769,17 +820,19 @@
             v(14, 8, 128),
             v(2, 14, 8, 128),
             v(7, SZ, 8, 128),
-            v(2, 8, 128),
-            v(2, 2, 8, 128),
+            v(4, 8, 128),
+            v(2, 4, 8, 128),
             v(4, 2 * SZ, 128),
+            pltpu.VMEM((3, 2 * SZ, 128), jnp.int32),
+            pltpu.VMEM((3, 8, 128), jnp.int32),
             pltpu.SemaphoreType.DMA((11,)),
             pltpu.SemaphoreType.DMA((8,)),
             pltpu.SemaphoreType.DMA((row,)),
             pltpu.SemaphoreType.DMA((row,)),
             pltpu.SemaphoreType.DMA((row,)),
             pltpu.SemaphoreType.DMA((row,)),
-            pltpu.SemaphoreType.DMA((18,)),
-            pltpu.SemaphoreType.DMA((18,)),
+            pltpu.SemaphoreType.DMA((20,)),
+            pltpu.SemaphoreType.DMA((20,)),
         ],
         compiler_params=pltpu.CompilerParams(
             collective_id=0, has_side_effects=True, vmem_limit_bytes=60 * 2**20

time: 55.6 us -> 52.1 us (0.937)
  Pallas kernels: 54.3 us -> 51.1 us
    pallas_call x1, Pallas kernels: 52.2 us -> 49 us  [shards(): pl.pallas_call(functools.partial(kernel, row, rows_tx), out_shape=jax.Sha...]
where the time goes in v1:
time: 52.1 us; the launch traced here: 51.9 us
  Pallas kernels  51.1 us (98%)
  between operations  0.8 us (2%)
    pallas_call x1, Pallas kernels, shards(): pl.pallas_call(functools.partial(kernel, row, rows_tx), out_shape=jax.Sha...  49 us
    pallas_call x1, Pallas kernels, shards(): pl.pallas_call(spread, out_shape=[jax.ShapeDtypeStruct(a.shape, F32) for...  2.12 us

profile of v1, /device:TPU:2, one launch (start us, length us, event | category | flops | bytes accessed | tf_op | source)
XLA Modules:
  0.0 51.9 jit_solution(15972717046915684338)
XLA Ops:
  0.6 49.0 %wind_step.1.far = f32[256,8,128]{2,1,0:T(8,128)} custom-call(f32[3,48,8,128]{3,2,1,0:T(8,128)} %far_vel.1, f32[48,8,128]{2,1,0:T(8,128)} %far_pre.1, f32[48,8,128]{2,1,0:T(8,128)} %far_drag.1, f32[2,48,8,128]{3,2,1,0:T(8,128)} %far_forc.1, f32[3,16,8,128]{3,2,1,0:T(8,128)} %far_svel.1, f32[16,8,128]{2,1,0:T(8,128)} %far_spre.1, f32[16,8,128]{2,1,0:T(8,128)} %far_sdrag.1, ...), custom_call_target="tpu_custom_call" | custom-call | tf_op jit(solution)/shard_map/wind_step/pallas_call | solution.py:774
  49.7 2.1 %spread.1 = (f32[3,48,8,128]{3,2,1,0:T(8,128)}, f32[48,8,128]{2,1,0:T(8,128)}, f32[3,16,8,128]{3,2,1,0:T(8,128)}, f32[16,8,128]{2,1,0:T(8,128)}) custom-call(f32[256,8,128]{2,1,0:T(8,128)} %wind_step.1.far), custom_call_target="tpu_custom_call" | custom-call | tf_op jit(solution)/shard_map/spread/pallas_call | solution.py:856
